TPU v7x, 32 devices: a whole 2x2x4 slice. The times are simulated.
32 devices in a mesh: blk: 4 (over y, x), grp: 8 (over z, core).
Axes of the slice: x: 2, y: 2, z: 4, core: 2. Of those that a mesh axis runs over, the one named last changes fastest.
Arguments:
- queries: bfloat16 [8, 128, 1280], P('blk'), may hold values from -8 to 8
- query_lengths: int32 [8], P('blk'), may hold values from 32 to 128, as said below
- targets: bfloat16 [128, 128, 1280], P(('blk', 'grp')), may hold values from -8 to 8
- target_lengths: int32 [128], P(('blk', 'grp')), may hold values from 32 to 128, as said below
Outputs:
- profile: float32 [8, 128, 1280], P('blk', 'grp')
- similarity: float32 [8, 128], P('blk', 'grp')
Inputs may be any that keep to these rules, and one draw needn't show every extreme that they name: The first query_lengths[q] residues of query q are valid, the rest is padding; some query has all 128. The first target_lengths[t] residues of target t are valid, the rest is padding; some target has all 128.
All inputs are finite; a program needn't handle non-finite values.
Results may differ from a plain program's by a relative error of at most 0.00079.
Values may be sent and summed in bfloat16 or wider, within the bound.
A program may use at most 64 MiB of HBM per device.

v0:
```python
import math

import jax
import jax.numpy as jnp
from jax import lax
from jax.sharding import PartitionSpec as P

STEPS = 3


def from_behind(array, axis, by):
    length = lax.axis_size(axis)
    return lax.ppermute(array, axis, [(i, (i + by) % length) for i in range(length)])


def align_pair(query_rows, query_len, target_rows, target_len):
    scale = 3.0 / math.sqrt(query_rows.shape[-1])
    scores = (
        jnp.einsum("qid,mjd->qmij", query_rows, target_rows, preferred_element_type=jnp.float32)
        * scale
    )
    positions = lax.broadcasted_iota(jnp.float32, (1, query_rows.shape[1]), 1)
    row_ok = positions < query_len[:, None]
    col_ok = positions < target_len[:, None]
    row_mask = row_ok[:, None, :, None]
    col_mask = col_ok[None, :, None, :]
    row_top = jnp.max(jnp.where(col_mask, scores, -jnp.inf), axis=3, keepdims=True)
    row_exp = jnp.where(col_mask, jnp.exp(scores - row_top), 0.0)
    row_soft = jnp.where(row_mask, row_exp / jnp.sum(row_exp, axis=3, keepdims=True), 0.0)
    col_top = jnp.max(jnp.where(row_mask, scores, -jnp.inf), axis=2, keepdims=True)
    col_exp = jnp.where(row_mask, jnp.exp(scores - col_top), 0.0)
    col_soft = jnp.where(col_mask, col_exp / jnp.sum(col_exp, axis=2, keepdims=True), 0.0)
    weights = row_soft + col_soft - row_soft * col_soft
    similarity = jnp.sum(weights * scores, axis=(2, 3)) / jnp.sum(weights, axis=(2, 3))
    profile = jnp.einsum(
        "qmij,mjd->qid",
        row_soft.astype(jnp.bfloat16),
        target_rows,
        preferred_element_type=jnp.float32,
    )
    return (similarity, profile)


def shards(queries, query_lengths, targets, target_lengths):
    blocks = targets.shape[0]
    group_size = lax.axis_size("grp")
    profile_scale = 1.0 / math.sqrt(group_size * blocks * (STEPS + 1))
    resident = (targets, target_lengths.astype(jnp.bfloat16))
    running = jnp.zeros(queries.shape, jnp.float32)
    arrived = [resident] + [
        from_behind((resident[0], resident[1]), "blk", offset) for offset in range(1, STEPS + 1)
    ]
    query_len = query_lengths.astype(jnp.float32)
    collected = []
    for visiting in arrived:
        pair_sim, pair_prof = align_pair(
            queries, query_len, visiting[0], visiting[1].astype(jnp.float32)
        )
        running = running + pair_prof
        collected.append(pair_sim)
    similarity = jnp.concatenate(collected, axis=1)
    shares = lax.psum_scatter(running, "grp", scatter_dimension=1, tiled=True) * profile_scale
    return (shares, similarity)


def solution(mesh):
    in_specs = (P("blk", None, None), P("blk"), P(("blk", "grp"), None, None), P(("blk", "grp")))
    out_specs = (P("blk", "grp", None), P("blk", "grp"))
    return jax.shard_map(shards, mesh=mesh, in_specs=in_specs, out_specs=out_specs, check_vma=False)
```

profile of v0, /device:TPU:0, one launch (start us, length us, event | category | flops | bytes accessed | tf_op | source)
XLA Modules:
  0.0 130.1 jit_solution(4620734244584439831)
XLA Ops:
  7.2 0.7 convert_convert_fusion
  7.9 3.0 %collective-permute-start.2 = (bf16[4]{0:T(256)(128)(2,1)S(1)}, bf16[4]{0:T(256)(128)(2,1)S(1)}, u32[]{:S(2)}, u32[]{:S(2)}) collective-permute-start(bf16[4]{0:T(256)(128)(2,1)S(1)} %get-tuple-element.13), channel_id=1, source_target_pairs={{0,16},{8,24},{16,0},{24,8},{1,17},{9,25},{17,1},{25,9},{2,18},{10... | collective-permute-start | bytes 32 | tf_op jit(solution)/shard_map/ppermute | solution.py:13
  10.9 1.5 %collective-permute-start = (bf16[4]{0:T(256)(128)(2,1)S(1)}, bf16[4]{0:T(256)(128)(2,1)S(1)}, u32[]{:S(2)}, u32[]{:S(2)}) collective-permute-start(bf16[4]{0:T(256)(128)(2,1)S(1)} %get-tuple-element.13), channel_id=1, source_target_pairs={{0,8},{8,16},{16,24},{24,0},{1,9},{9,17},{17,25},{25,1},{2,10},{10... | collective-permute-start | bytes 32 | tf_op jit(solution)/shard_map/ppermute | solution.py:13
  12.4 1.4 %collective-permute-start.4 = (bf16[4]{0:T(256)(128)(2,1)S(1)}, bf16[4]{0:T(256)(128)(2,1)S(1)}, u32[]{:S(2)}, u32[]{:S(2)}) collective-permute-start(bf16[4]{0:T(256)(128)(2,1)S(1)} %get-tuple-element.13), channel_id=1, source_target_pairs={{0,24},{8,0},{16,8},{24,16},{1,25},{9,1},{17,9},{25,17},{2,26},{10... | collective-permute-start | bytes 32 | tf_op jit(solution)/shard_map/ppermute | solution.py:13
  13.8 0.6 collective-permute-start.1
  14.4 2.3 %collective-permute-start.5 = (bf16[4,128,1280]{2,1,0:T(8,128)(2,1)}, bf16[4,128,1280]{2,1,0:T(8,128)(2,1)S(1)}, u32[]{:S(2)}, u32[]{:S(2)}) collective-permute-start(bf16[4,128,1280]{2,1,0:T(8,128)(2,1)} %param.6), channel_id=1, source_target_pairs={{0,24},{8,0},{16,8},{24,16},{1,25},{9,1},{17,9},{25,17},{2,26},{10... | collective-permute-start | bytes 3932168 | tf_op jit(solution)/shard_map/ppermute | solution.py:13
  16.8 0.7 convert_element_type.30
  17.5 2.0 %fusion.38 = f32[2,4,128,128]{2,3,0,1:T(8,128)S(1)} fusion(bf16[4,128,1280]{2,1,0:T(8,128)(2,1)} %param.6, bf16[2,128,1280]{2,1,0:T(8,128)(2,1)S(1)} %copy-done), kind=kOutput, calls=%fused_computation.40 | convolution fusion | flops 335675392 | bytes 2490368 | tf_op jit(solution)/shard_map/qid,mjd->qmij/dot_general | solution.py:19
  19.5 0.6 fusion.164
  20.1 0.5 convolution_bitcast_fusion.3
  21.1 25.6 %collective-permute-done.1 = bf16[4,128,1280]{2,1,0:T(8,128)(2,1)S(1)} collective-permute-done((bf16[4,128,1280]{2,1,0:T(8,128)(2,1)}, bf16[4,128,1280]{2,1,0:T(8,128)(2,1)S(1)}, u32[]{:S(2)}, u32[]{:S(2)}) %collective-permute-start.1) | collective-permute-done | bytes 1310752 | tf_op jit(solution)/shard_map/ppermute | solution.py:13
  46.7 0.5 fusion.44
  47.3 0.5 copy-done.18
  47.8 1.6 %fusion.165 = (f32[2,4,128]{2,0,1:T(2,128)}, f32[2,4,128,128]{2,3,0,1:T(8,128)}) fusion(f32[2,4,128,128]{2,3,0,1:T(8,128)S(1)} %fusion.44, pred[4,128]{1,0:T(4,128)(4,1)S(1)} %iota_compare_fusion.2), kind=kOutput, calls=%fused_computation.159 | output fusion | flops 524415 | bytes 1053184 | tf_op jit(solution)/shard_map/sub | solution.py:28
  49.4 22.2 %collective-permute-done.5 = bf16[4,128,1280]{2,1,0:T(8,128)(2,1)S(1)} collective-permute-done((bf16[4,128,1280]{2,1,0:T(8,128)(2,1)}, bf16[4,128,1280]{2,1,0:T(8,128)(2,1)S(1)}, u32[]{:S(2)}, u32[]{:S(2)}) %collective-permute-start.5) | collective-permute-done | bytes 1310752 | tf_op jit(solution)/shard_map/ppermute | solution.py:13
  71.6 0.5 fusion.56
  72.2 0.5 copy-done.2
  72.7 0.6 fusion.163
  73.3 0.5 fusion.50
  73.9 0.5 copy-done.3
  74.4 1.0 fusion.166
  75.4 3.5 %fusion.14 = f32[2,128,1280]{2,1,0:T(8,128)} fusion(f32[2,128,1280]{2,1,0:T(8,128)S(1)} %convolution_bitcast_fusion.3, bf16[4,128,1280]{2,1,0:T(8,128)(2,1)} %copy-done.18, f32[2,4,128]{2,0,1:T(2,128)} %get-tuple-element.18, pred[2,128]{1,0:T(4,128)(4,1)S(1)} %iota_compare_fusion.4, f32[2,4,128,128]{2,3,0,1:T(8,128)} %copy-done.7, pred[4,128]{1,0:T(4,128)(4,1)} %copy-done.16), kind=kOutput, calls=%fused_computation.17 | convolution fusion | flops 336659584 | bytes 4461312 | tf_op jit(solution)/shard_map/qmij,mjd->qid/dot_general | solution.py:35
  78.9 1.9 %convolution_bitcast_fusion = f32[2,128,1280]{2,1,0:T(8,128)S(1)} fusion(bf16[4,128,1280]{2,1,0:T(8,128)(2,1)} %copy-done.2, f32[2,4,128,128]{2,3,0,1:T(8,128)S(1)} %get-tuple-element.15, f32[2,4,128]{2,0,1:T(2,128)S(1)} %get-tuple-element.14, pred[2,128]{1,0:T(4,128)(4,1)S(1)} %iota_compare_fusion.4), kind=kOutput, calls=%fused_computation.12 | convolution fusion | flops 335937536 | bytes 3150080 | tf_op jit(solution)/shard_map/qmij,mjd->qid/dot_general | solution.py:35
  80.8 3.6 %fusion.13 = f32[2,128,1280]{2,1,0:T(8,128)} fusion(f32[2,128,1280]{2,1,0:T(8,128)S(1)} %convolution_bitcast_fusion, f32[2,128,1280]{2,1,0:T(8,128)} %fusion.14, bf16[4,128,1280]{2,1,0:T(8,128)(2,1)} %copy-done.3, f32[2,4,128]{2,0,1:T(2,128)S(1)} %get-tuple-element.20, pred[2,128]{1,0:T(4,128)(4,1)S(1)} %iota_compare_fusion.4, ...), kind=kOutput, calls=%fused_computation.15 | convolution fusion | flops 336987264 | bytes 5772032 | tf_op jit(solution)/shard_map/qmij,mjd->qid/dot_general | solution.py:35
  84.4 0.5 copy-done.13
  84.9 2.5 %fusion.159 = (f32[2,4]{0,1:T(4,128)S(1)}, f32[2,4]{0,1:T(4,128)S(1)}) fusion(f32[2,4,128,128]{2,3,0,1:T(8,128)} %copy-done.4, pred[2,128]{1,0:T(4,128)(4,1)S(1)} %iota_compare_fusion.4, pred[4,128]{1,0:T(4,128)(4,1)S(1)} %copy-done.13, f32[2,4,128,128]{2,3,0,1:T(8,128)S(1)} %get-tuple-element.17, f32[2,4,128]{2,0,1:T(2,128)S(1)} %get-tuple-element.16), kind=kOutput, calls=%fused_computation.153 | output fusion | flops 1706222 | bytes 1053504 | tf_op jit(solution)/shard_map/div | solution.py:32
  87.6 2.7 %fusion.160 = (f32[2,4]{0,1:T(4,128)S(1)}, f32[2,4]{0,1:T(4,128)S(1)}) fusion(f32[2,4,128,128]{2,3,0,1:T(8,128)} %copy-done.7, pred[2,128]{1,0:T(4,128)(4,1)S(1)} %iota_compare_fusion.4, pred[4,128]{1,0:T(4,128)(4,1)S(1)} %copy-done.17, f32[2,4,128,128]{2,3,0,1:T(8,128)S(1)} %copy-done.8, f32[2,4,128]{2,0,1:T(2,128)S(1)} %copy-done.9), kind=kOutput, calls=%fused_computation.154 | output fusion | flops 1706222 | bytes 1053504 | tf_op jit(solution)/shard_map/div | solution.py:32
  90.4 2.6 %fusion.162 = (f32[2,4]{0,1:T(4,128)S(1)}, f32[2,4]{0,1:T(4,128)S(1)}) fusion(f32[2,4,128,128]{2,3,0,1:T(8,128)} %copy-done.6, pred[2,128]{1,0:T(4,128)(4,1)S(1)} %iota_compare_fusion.4, pred[4,128]{1,0:T(4,128)(4,1)S(1)} %copy-done.15, f32[2,4,128,128]{2,3,0,1:T(8,128)S(1)} %get-tuple-element.15, f32[2,4,128]{2,0,1:T(2,128)S(1)} %get-tuple-element.14), kind=kOutput, calls=%fused_computation.156 | output fusion | flops 1706222 | bytes 1053504 | tf_op jit(solution)/shard_map/div | solution.py:32
  93.2 1.1 fusion.161
  94.4 0.7 pad_maximum_fusion
  95.0 26.6 %reduce-scatter.2.cloned.1.call-done = f32[2,16,1280]{2,1,0:T(8,128)} async-done(((f32[2,128,1280]{2,1,0:T(8,128)}), f32[2,16,1280]{2,1,0:T(8,128)}) %reduce-scatter.2.cloned.1.call-update) | async-done | bytes 163856 | tf_op jit(solution)/shard_map/reduce_scatter | solution.py:62
  121.6 1.6 %broadcast_multiply_fusion = f32[2,16,1280]{2,1,0:T(8,128)} fusion(f32[2,16,1280]{2,1,0:T(8,128)} %reduce-scatter.2.cloned.1.call-done), kind=kLoop, calls=%fused_computation.123 | loop fusion | flops 40960 | bytes 327680 | tf_op jit(solution)/shard_map/mul | solution.py:62
  (57 shorter events, 1.0 us)
Async XLA Ops:
  7.2 10.3 %copy-start = (bf16[2,128,1280]{2,1,0:T(8,128)(2,1)S(1)}, bf16[2,128,1280]{2,1,0:T(8,128)(2,1)}, u32[]{:S(2)}) copy-start(bf16[2,128,1280]{2,1,0:T(8,128)(2,1)} %param.4) | copy-start | bytes 1966084
  7.2 114.4 %reduce-scatter.2.cloned.1.call-start = ((), (), s32[]{:S(2)}) async-start(), calls=%async_computation.1 | async-start | bytes 1474560 | tf_op jit(solution)/shard_map/reduce_scatter | solution.py:62
  7.9 12.8 %collective-permute-start.2 = (bf16[4]{0:T(256)(128)(2,1)S(1)}, bf16[4]{0:T(256)(128)(2,1)S(1)}, u32[]{:S(2)}, u32[]{:S(2)}) collective-permute-start(bf16[4]{0:T(256)(128)(2,1)S(1)} %get-tuple-element.13), channel_id=1, source_target_pairs={{0,16},{8,24},{16,0},{24,8},{1,17},{9,25},{17,1},{25,9},{2,18},{10... | collective-permute-start | bytes 32 | tf_op jit(solution)/shard_map/ppermute | solution.py:13
  10.9 9.9 %collective-permute-start = (bf16[4]{0:T(256)(128)(2,1)S(1)}, bf16[4]{0:T(256)(128)(2,1)S(1)}, u32[]{:S(2)}, u32[]{:S(2)}) collective-permute-start(bf16[4]{0:T(256)(128)(2,1)S(1)} %get-tuple-element.13), channel_id=1, source_target_pairs={{0,8},{8,16},{16,24},{24,0},{1,9},{9,17},{17,25},{25,1},{2,10},{10... | collective-permute-start | bytes 32 | tf_op jit(solution)/shard_map/ppermute | solution.py:13
  12.4 8.6 %collective-permute-start.4 = (bf16[4]{0:T(256)(128)(2,1)S(1)}, bf16[4]{0:T(256)(128)(2,1)S(1)}, u32[]{:S(2)}, u32[]{:S(2)}) collective-permute-start(bf16[4]{0:T(256)(128)(2,1)S(1)} %get-tuple-element.13), channel_id=1, source_target_pairs={{0,24},{8,0},{16,8},{24,16},{1,25},{9,1},{17,9},{25,17},{2,26},{10... | collective-permute-start | bytes 32 | tf_op jit(solution)/shard_map/ppermute | solution.py:13
  13.8 32.9 %collective-permute-start.1 = (bf16[4,128,1280]{2,1,0:T(8,128)(2,1)}, bf16[4,128,1280]{2,1,0:T(8,128)(2,1)S(1)}, u32[]{:S(2)}, u32[]{:S(2)}) collective-permute-start(bf16[4,128,1280]{2,1,0:T(8,128)(2,1)} %param.6), channel_id=1, source_target_pairs={{0,8},{8,16},{16,24},{24,0},{1,9},{9,17},{17,25},{25,1},{2,10},{10... | collective-permute-start | bytes 3932168 | tf_op jit(solution)/shard_map/ppermute | solution.py:13
  14.4 57.2 %collective-permute-start.5 = (bf16[4,128,1280]{2,1,0:T(8,128)(2,1)}, bf16[4,128,1280]{2,1,0:T(8,128)(2,1)S(1)}, u32[]{:S(2)}, u32[]{:S(2)}) collective-permute-start(bf16[4,128,1280]{2,1,0:T(8,128)(2,1)} %param.6), channel_id=1, source_target_pairs={{0,24},{8,0},{16,8},{24,16},{1,25},{9,1},{17,9},{25,17},{2,26},{10... | collective-permute-start | bytes 3932168 | tf_op jit(solution)/shard_map/ppermute | solution.py:13
  17.5 2.6 %copy-start.1 = (bf16[4,128,1280]{2,1,0:T(8,128)(2,1)S(1)}, bf16[4,128,1280]{2,1,0:T(8,128)(2,1)}, u32[]{:S(2)}) copy-start(bf16[4,128,1280]{2,1,0:T(8,128)(2,1)} %param.6) | copy-start | bytes 3932164
  19.5 1.2 copy-start.4
  19.5 1.1 copy-start.12
  20.7 52.6 %collective-permute-start.3 = (bf16[4,128,1280]{2,1,0:T(8,128)(2,1)S(1)}, bf16[4,128,1280]{2,1,0:T(8,128)(2,1)S(1)}, u32[]{:S(2)}, u32[]{:S(2)}) collective-permute-start(bf16[4,128,1280]{2,1,0:T(8,128)(2,1)S(1)} %copy-done.1), channel_id=1, source_target_pairs={{0,16},{8,24},{16,0},{24,8},{1,17},{9,25},{17,1},{25,9},{2,18},{10... | collective-permute-start | bytes 3932168 | tf_op jit(solution)/shard_map/ppermute | solution.py:13
  20.9 52.9 %copy-start.10 = (pred[4,128]{1,0:T(4,128)(4,1)}, pred[4,128]{1,0:T(4,128)(4,1)S(1)}, u32[]{:S(2)}) copy-start(pred[4,128]{1,0:T(4,128)(4,1)S(1)} %iota_compare_fusion.1) | copy-start | bytes 1540
  21.0 26.3 %copy-start.16 = (pred[4,128]{1,0:T(4,128)(4,1)}, pred[4,128]{1,0:T(4,128)(4,1)S(1)}, u32[]{:S(2)}) copy-start(pred[4,128]{1,0:T(4,128)(4,1)S(1)} %iota_compare_fusion.2) | copy-start | bytes 1540
  21.1 51.1 %copy-start.14 = (pred[4,128]{1,0:T(4,128)(4,1)}, pred[4,128]{1,0:T(4,128)(4,1)S(1)}, u32[]{:S(2)}) copy-start(pred[4,128]{1,0:T(4,128)(4,1)S(1)} %iota_compare_fusion) | copy-start | bytes 1540
  46.7 1.1 copy-start.18
  47.8 24.4 %copy-start.7 = (f32[2,4,128,128]{2,3,0,1:T(8,128)}, f32[2,4,128,128]{2,3,0,1:T(8,128)S(1)}, u32[]{:S(2)}) copy-start(f32[2,4,128,128]{2,3,0,1:T(8,128)S(1)} %fusion.44) | copy-start | bytes 1572868
  71.6 1.1 copy-start.2
  72.7 1.2 copy-start.6
  73.3 1.1 copy-start.3
  84.4 0.6 copy-start.13
  84.9 2.7 %copy-start.8 = (f32[2,4,128,128]{2,3,0,1:T(8,128)S(1)}, f32[2,4,128,128]{2,3,0,1:T(8,128)}, u32[]{:S(2)}) copy-start(f32[2,4,128,128]{2,3,0,1:T(8,128)} %get-tuple-element.19) | copy-start | bytes 1572868
  84.9 2.7 %copy-start.9 = (f32[2,4,128]{2,0,1:T(2,128)S(1)}, f32[2,4,128]{2,0,1:T(2,128)}, u32[]{:S(2)}) copy-start(f32[2,4,128]{2,0,1:T(2,128)} %get-tuple-element.18) | copy-start | bytes 12292
  84.9 2.7 %copy-start.17 = (pred[4,128]{1,0:T(4,128)(4,1)S(1)}, pred[4,128]{1,0:T(4,128)(4,1)}, u32[]{:S(2)}) copy-start(pred[4,128]{1,0:T(4,128)(4,1)} %copy-done.16) | copy-start | bytes 1540
  87.6 2.8 %copy-start.15 = (pred[4,128]{1,0:T(4,128)(4,1)S(1)}, pred[4,128]{1,0:T(4,128)(4,1)}, u32[]{:S(2)}) copy-start(pred[4,128]{1,0:T(4,128)(4,1)} %copy-done.14) | copy-start | bytes 1540
  90.4 2.8 %copy-start.5 = (f32[2,4,128,128]{2,3,0,1:T(8,128)S(1)}, f32[2,4,128,128]{2,3,0,1:T(8,128)}, u32[]{:S(2)}) copy-start(f32[2,4,128,128]{2,3,0,1:T(8,128)} %get-tuple-element.21) | copy-start | bytes 1572868
  90.4 2.8 %copy-start.11 = (pred[4,128]{1,0:T(4,128)(4,1)S(1)}, pred[4,128]{1,0:T(4,128)(4,1)}, u32[]{:S(2)}) copy-start(pred[4,128]{1,0:T(4,128)(4,1)} %copy-done.10) | copy-start | bytes 1540
Sparse Core Ops, SparseCore 0:
  84.5 37.0 reduce-scatter.1
where the time goes:
time: 130 us
  waiting for transfers between devices  74.4 us (57%)
  other arithmetic  16.8 us (13%)
  between operations  14.3 us (11%)
  matrix products  13.1 us (10%)
  starting transfers between devices  8.95 us (7%)
  local copies, waits for them, and re-layouts  2.51 us (2%)
    ppermute x6, waiting for transfers between devices, from_behind(): lax.ppermute(array, axis, [(i, (i + by) % length) for i in range(length)])  47.8 us
    reduce_scatter x1, waiting for transfers between devices, shards(): lax.psum_scatter(running, 'grp', scatter_dimension=1, tiled=True)  26.6 us
    dot_general x4, matrix products, align_pair(): jnp.einsum('qmij,mjd->qid', row_soft.astype(jnp.bfloat16), target_rows, p...  9.53 us
    div x4, other arithmetic, align_pair(): col_exp / jnp.sum(col_exp, axis=2, keepdims=True)  8.97 us
    ppermute x6, starting transfers between devices, from_behind(): lax.ppermute(array, axis, [(i, (i + by) % length) for i in range(length)])  8.92 us
    sub x4, other arithmetic, align_pair(): row_exp = jnp.where(col_mask, jnp.exp(scores - row_top), 0.0)  3.79 us
    dot_general x4, matrix products, align_pair(): jnp.einsum('qid,mjd->qmij', query_rows, target_rows, preferred_element_ty...  3.58 us
  transfers between devices with their start and end apart: 7, of which 3 were waited for; matrix products, arithmetic and copies ran while one was open for 13% of the time, Pallas kernels for 0%

commit v1 on v0

--- a/solution.py
+++ b/solution.py
@@ -1,11 +1,16 @@
+import functools
 import math
 
 import jax
 import jax.numpy as jnp
 from jax import lax
+from jax.experimental import pallas as pl
+from jax.experimental.pallas import tpu as pltpu
 from jax.sharding import PartitionSpec as P
 
 STEPS = 3
+MESH = pl.DeviceIdType.MESH
+LOW = -1e30
 
 
 def from_behind(array, axis, by):
@@ -41,7 +46,7 @@
     return (similarity, profile)
 
 
-def shards(queries, query_lengths, targets, target_lengths):
+def ring_shards(queries, query_lengths, targets, target_lengths):
     blocks = targets.shape[0]
     group_size = lax.axis_size("grp")
     profile_scale = 1.0 / math.sqrt(group_size * blocks * (STEPS + 1))
@@ -63,7 +68,285 @@
     return (shares, similarity)
 
 
+def remote(src, dst, sems, k, device):
+    return pltpu.make_async_remote_copy(
+        src_ref=src,
+        dst_ref=dst,
+        send_sem=sems.at[0, k],
+        recv_sem=sems.at[1, k],
+        device_id=device,
+        device_id_type=MESH,
+    )
+
+
+def kernel(
+    scale, profile_scale,
+    ql_ref, tl_ref, q_hbm, t_hbm, prof_ref, sim_ref,
+    q_buf, t_buf, ql_buf, tl_buf, a_buf, r_buf, rx_a, rx_b, rx_c, rx_z, tx_s, rx_s,
+    local_sems, q_sems, l_sems, r_sems, z_sems, s_sems,
+):
+    res, wide = q_buf.shape[1:]
+    per_core = t_buf.shape[1]
+    blk, grp = lax.axis_index("blk"), lax.axis_index("grp")
+    x, y = blk % 2, blk // 2
+    c, z = grp % 2, grp // 2
+    other_x, other_y = y * 2 + (1 - x), (1 - y) * 2 + x
+    near = other_x * (1 - c) + other_y * c
+    far = other_y * (1 - c) + other_x * c
+    blks = (blk, near, far, 3 - blk)
+    sibling = z * 2 + (1 - c)
+
+    barrier = pltpu.get_barrier_semaphore()
+    partners = [(b, grp) for b in blks[1:]] + [(b, sibling) for b in blks]
+    for step in range(1, 4):
+        there = (z + step) % 4
+        partners += [(blk, there * 2 + c), (blk, there * 2 + (1 - c))]
+    for partner in partners:
+        pl.semaphore_signal(barrier, inc=1, device_id=partner, device_id_type=MESH)
+
+    load_q = pltpu.make_async_copy(q_hbm.at[c], q_buf.at[0], local_sems.at[0])
+    load_t = pltpu.make_async_copy(t_hbm, t_buf.at[0], local_sems.at[1])
+    load_q.start()
+    load_t.start()
+    ql_buf[0] = jnp.full((8, 128), ql_ref[c], jnp.int32)
+    line = lax.broadcasted_iota(jnp.int32, (8, 128), 0)
+    lengths = jnp.zeros((8, 128), jnp.int32)
+    for r in range(per_core):
+        lengths = jnp.where(line == r, tl_ref[r], lengths)
+    tl_buf[0] = lengths
+    pl.semaphore_wait(barrier, len(partners))
+
+    send_near = remote(q_hbm.at[c], q_buf.at[1], q_sems, 0, (near, grp))
+    send_far = remote(q_hbm.at[c], q_buf.at[2], q_sems, 1, (far, grp))
+    send_t = remote(t_hbm, t_buf.at[1], q_sems, 3, (blk, sibling))
+    pass_on = remote(q_buf.at[1], q_buf.at[3], q_sems, 2, (far, grp))
+    send_near.start()
+    send_far.start()
+    send_t.start()
+    send_len = [
+        remote(ql_buf.at[0], ql_buf.at[s], l_sems, s - 1, (blks[s], grp)) for s in range(1, 4)
+    ]
+    send_len.append(remote(tl_buf.at[0], tl_buf.at[1], l_sems, 3, (blk, sibling)))
+    for copy in send_len:
+        copy.start()
+
+    lane = lax.broadcasted_iota(jnp.int32, (8, 128), 1)
+    col_at = lax.broadcasted_iota(jnp.int32, (res, res), 1)
+    row_at = lax.broadcasted_iota(jnp.int32, (res, res), 0)
+
+    def align(s, h):
+        scores_all = lax.dot_general(
+            q_buf[s],
+            t_buf[h].reshape(per_core * res, wide),
+            (((1,), (1,)), ((), ())),
+            preferred_element_type=jnp.float32,
+        ) * scale
+        row_ok = row_at < ql_buf[s, 0:1, :]
+        row_ok_vec = row_ok[:, 0:1]
+        place = ((blks[s] - blk + 4) % 4) * per_core
+        tile = jnp.zeros((8, 128), jnp.float32)
+        for r in range(per_core):
+            scores = scores_all[:, r * res : (r + 1) * res]
+            col_ok = col_at < tl_buf[h, r : r + 1, :]
+            by_row = jnp.where(col_ok, scores, LOW)
+            row_exp = jnp.exp(by_row - jnp.max(by_row, axis=1, keepdims=True))
+            row_inv = jnp.where(row_ok_vec, 1.0 / jnp.sum(row_exp, axis=1, keepdims=True), 0.0)
+            row_soft = row_exp * row_inv
+            by_col = jnp.where(row_ok, scores, LOW)
+            col_exp = jnp.exp(by_col - jnp.max(by_col, axis=0, keepdims=True))
+            col_inv = jnp.where(
+                col_ok[0:1, :], 1.0 / jnp.sum(col_exp, axis=0, keepdims=True), 0.0
+            )
+            col_soft = col_exp * col_inv
+            weights = row_soft + col_soft - row_soft * col_soft
+            upper = jnp.sum(
+                jnp.sum(weights * scores, axis=0, keepdims=True), axis=1, keepdims=True
+            )
+            lower = jnp.sum(jnp.sum(weights, axis=0, keepdims=True), axis=1, keepdims=True)
+            tile = jnp.where((line == c) & (lane == place + r), upper / lower, tile)
+            a_buf[h, :, r * res : (r + 1) * res] = row_soft.astype(jnp.bfloat16)
+        tx_s[s, h] = tile
+
+    def profile(s):
+        step = 256
+
+        def body(n, carry):
+            cols = pl.ds(pl.multiple_of(n * step, step), step)
+            r_buf[s, :, cols] = sum(
+                jnp.dot(
+                    a_buf[h],
+                    t_buf[h, :, :, cols].reshape(per_core * res, step),
+                    preferred_element_type=jnp.float32,
+                )
+                for h in range(2)
+            )
+            return carry
+
+        lax.fori_loop(0, wide // step, body, 0)
+
+    def both(s):
+        def body(h, carry):
+            align(s, h)
+            return carry
+
+        lax.fori_loop(0, 2, body, 0)
+        profile(s)
+
+    def send_sim(s):
+        out = []
+        for h in range(2):
+            if s or h:
+                copy = remote(
+                    tx_s.at[s, h], rx_s.at[s, h], s_sems, s * 2 + h,
+                    (blks[s], sibling if h else grp),
+                )
+                copy.start()
+                out.append(copy)
+        return out
+
+    load_q.wait()
+    load_t.wait()
+    send_t.wait_recv()
+    send_len[3].wait_recv()
+    both(0)
+    sims = send_sim(0)
+
+    send_near.wait_recv()
+    pass_on.start()
+    send_len[0].wait_recv()
+    both(1)
+    send_a = remote(r_buf.at[1], rx_a, r_sems, 0, (near, grp))
+    send_a.start()
+    sims += send_sim(1)
+
+    send_far.wait_recv()
+    send_len[1].wait_recv()
+    both(2)
+    sims += send_sim(2)
+
+    pass_on.wait_recv()
+    send_len[2].wait_recv()
+    both(3)
+
+    quarter = res // 4
+    half = quarter // 2
+
+    def chunk(i):
+        return (z + 1 + i) % 4
+
+    def rows(i):
+        return pl.ds(pl.multiple_of(chunk(i) * quarter, quarter), quarter)
+
+    send_b, send_c, send_z = [], [], []
+    for i in range(4):
+        send_b.append(
+            remote(r_buf.at[3, rows(i)], rx_b.at[rows(i)], r_sems, 1 + i, (near, grp))
+        )
+        send_b[i].start()
+    sims += send_sim(3)
+
+    def finish(i):
+        if i == 0:
+            send_a.wait_recv()
+        send_c[i].wait_recv()
+        r_buf[0, rows(i), :] = r_buf[0, rows(i), :] + rx_a[rows(i), :] + rx_c[rows(i), :]
+        for u in range(2):
+            core = 1 - c if u else c
+            there = chunk(i) * 2 + core
+            if i < 3 or u:
+                mine = pl.ds(pl.multiple_of(there * half, half), half)
+                copy = remote(
+                    r_buf.at[0, mine], rx_z.at[i, u], z_sems, i * 2 + u, (blk, there)
+                )
+                copy.start()
+                send_z.append(copy)
+
+    for i in range(4):
+        send_b[i].wait_recv()
+        r_buf[2, rows(i), :] = r_buf[2, rows(i), :] + rx_b[rows(i), :]
+        send_c.append(
+            remote(r_buf.at[2, rows(i)], rx_c.at[rows(i)], r_sems, 5 + i, (far, grp))
+        )
+        send_c[i].start()
+        if i:
+            finish(i - 1)
+    finish(3)
+
+    total = tx_s[0, 0]
+    for copy in sims:
+        copy.wait_recv()
+    for s in range(4):
+        for h in range(2):
+            if s or h:
+                total = total + rx_s[s, h]
+    sim_ref[...] = total[0:2, 0 : sim_ref.shape[1]]
+
+    for copy in send_z:
+        copy.wait_recv()
+    own = pl.ds(pl.multiple_of(grp * half, half), half)
+    prof_ref[c] = (
+        r_buf[0, own, :] + rx_z[0, 0] + rx_z[1, 0] + rx_z[2, 0]
+    ) * profile_scale
+    prof_ref[1 - c] = (
+        rx_z[0, 1] + rx_z[1, 1] + rx_z[2, 1] + rx_z[3, 1]
+    ) * profile_scale
+
+    for copy in (
+        [send_near, send_far, send_t, pass_on, send_a] + send_len + sims + send_b + send_c + send_z
+    ):
+        copy.wait_send()
+
+
+def plane_shards(queries, query_lengths, targets, target_lengths):
+    sets, res, wide = queries.shape
+    per_core = targets.shape[0]
+    scale = 3.0 / math.sqrt(wide)
+    profile_scale = 1.0 / math.sqrt(lax.axis_size("grp") * per_core * (STEPS + 1))
+    part = res // lax.axis_size("grp")
+    f32, bf16 = jnp.float32, jnp.bfloat16
+    vmem = pltpu.VMEM
+    return pl.pallas_call(
+        functools.partial(kernel, scale, profile_scale),
+        out_shape=(
+            jax.ShapeDtypeStruct((sets, part, wide), f32),
+            jax.ShapeDtypeStruct((sets, (STEPS + 1) * per_core), f32),
+        ),
+        in_specs=[
+            pl.BlockSpec(memory_space=pltpu.SMEM),
+            pl.BlockSpec(memory_space=pltpu.SMEM),
+            pl.BlockSpec(memory_space=pl.ANY),
+            pl.BlockSpec(memory_space=pl.ANY),
+        ],
+        out_specs=(pl.BlockSpec(memory_space=vmem), pl.BlockSpec(memory_space=vmem)),
+        scratch_shapes=[
+            vmem((4, res, wide), bf16),
+            vmem((2, per_core, res, wide), bf16),
+            vmem((4, 8, 128), jnp.int32),
+            vmem((2, 8, 128), jnp.int32),
+            vmem((2, res, per_core * res), bf16),
+            vmem((4, res, wide), f32),
+            vmem((res, wide), f32),
+            vmem((res, wide), f32),
+            vmem((res, wide), f32),
+            vmem((4, 2, part, wide), f32),
+            vmem((4, 2, 8, 128), f32),
+            vmem((4, 2, 8, 128), f32),
+            pltpu.SemaphoreType.DMA((2,)),
+            pltpu.SemaphoreType.DMA((2, 4)),
+            pltpu.SemaphoreType.DMA((2, 4)),
+            pltpu.SemaphoreType.DMA((2, 9)),
+            pltpu.SemaphoreType.DMA((2, 8)),
+            pltpu.SemaphoreType.DMA((2, 8)),
+        ],
+        compiler_params=pltpu.CompilerParams(
+            collective_id=0, has_side_effects=True, vmem_limit_bytes=40 * 1024 * 1024
+        ),
+    )(query_lengths, target_lengths, queries, targets)
+
+
 def solution(mesh):
     in_specs = (P("blk", None, None), P("blk"), P(("blk", "grp"), None, None), P(("blk", "grp")))
     out_specs = (P("blk", "grp", None), P("blk", "grp"))
+    plane = mesh.shape["blk"] == STEPS + 1 == 4 and mesh.shape["grp"] == 8
+    shards = plane_shards if plane else ring_shards
     return jax.shard_map(shards, mesh=mesh, in_specs=in_specs, out_specs=out_specs, check_vma=False)

time: 130 us -> 56.7 us (0.44)
  the two profiles are of different devices: /device:TPU:0 before, /device:TPU:9 now
where the time goes in v1:
time: 56.7 us; the launch traced here: 56.5 us
  Pallas kernels  50.9 us (90%)
  local copies, waits for them, and re-layouts  4.94 us (9%)
  between operations  0.65 us (1%)
    pallas_call x1, Pallas kernels, plane_shards(): pl.pallas_call(functools.partial(kernel, scale, profile_scale), out_shape...  50.9 us
    unnamed x10, local copies, waits for them, and re-layouts  4.94 us

profile of v1, /device:TPU:9, one launch (start us, length us, event | category | flops | bytes accessed | tf_op | source)
XLA Modules:
  0.0 56.5 jit_solution(2872236694643928190)
XLA Ops:
  0.6 0.0 copy-start
  0.6 1.3 %copy-done = bf16[4,128,1280]{2,1,0:T(8,128)(2,1)S(1)} copy-done((bf16[4,128,1280]{2,1,0:T(8,128)(2,1)S(1)}, bf16[4,128,1280]{2,1,0:T(8,128)(2,1)}, u32[]{:S(2)}) %copy-start) | copy-done | bytes 1310744
  1.9 0.0 copy-start.1
  1.9 1.1 %copy-done.1 = bf16[2,128,1280]{2,1,0:T(8,128)(2,1)S(1)} copy-done((bf16[2,128,1280]{2,1,0:T(8,128)(2,1)S(1)}, bf16[2,128,1280]{2,1,0:T(8,128)(2,1)}, u32[]{:S(2)}) %copy-start.1) | copy-done | bytes 655384
  3.0 0.0 copy-start.2
  3.0 0.7 %copy-done.2 = s32[2]{0:T(128)S(1)} copy-done((s32[2]{0:T(128)S(1)}, s32[2]{0:T(128)}, u32[]{:S(2)}) %copy-start.2) | copy-done | bytes 32
  3.7 0.0 copy-start.3
  3.7 0.7 %copy-done.3 = s32[4]{0:T(128)S(1)} copy-done((s32[4]{0:T(128)S(1)}, s32[4]{0:T(128)}, u32[]{:S(2)}) %copy-start.3) | copy-done | bytes 40
  4.3 50.9 %shard_map.59 = (f32[2,16,1280]{2,1,0:T(8,128)S(1)}, f32[2,16]{1,0:T(2,128)S(1)}) custom-call(s32[2]{0:T(128)S(1)} %copy-done.2, s32[4]{0:T(128)S(1)} %copy-done.3, bf16[2,128,1280]{2,1,0:T(8,128)(2,1)S(1)} %copy-done.1, bf16[4,128,1280]{2,1,0:T(8,128)(2,1)S(1)} %copy-done), custom_call_target="tpu_custom_call" | custom-call | tf_op jit(solution)/shard_map/pallas_call | solution.py:308
  55.3 0.7 %copy.8 = f32[2,16,1280]{2,1,0:T(8,128)} copy(f32[2,16,1280]{2,1,0:T(8,128)S(1)} %get-tuple-element.4) | data formatting | bytes 327680
  56.0 0.6 copy.9
Async XLA Ops:
  0.6 1.3 %copy-start = (bf16[4,128,1280]{2,1,0:T(8,128)(2,1)S(1)}, bf16[4,128,1280]{2,1,0:T(8,128)(2,1)}, u32[]{:S(2)}) copy-start(bf16[4,128,1280]{2,1,0:T(8,128)(2,1)} %t_hbm.1) | copy-start | bytes 3932164
  1.9 1.1 %copy-start.1 = (bf16[2,128,1280]{2,1,0:T(8,128)(2,1)S(1)}, bf16[2,128,1280]{2,1,0:T(8,128)(2,1)}, u32[]{:S(2)}) copy-start(bf16[2,128,1280]{2,1,0:T(8,128)(2,1)} %q_hbm.1) | copy-start | bytes 1966084
  3.0 0.7 %copy-start.2 = (s32[2]{0:T(128)S(1)}, s32[2]{0:T(128)}, u32[]{:S(2)}) copy-start(s32[2]{0:T(128)} %ql_ref.1) | copy-start | bytes 28
  3.7 0.7 %copy-start.3 = (s32[4]{0:T(128)S(1)}, s32[4]{0:T(128)}, u32[]{:S(2)}) copy-start(s32[4]{0:T(128)} %tl_ref.1) | copy-start | bytes 52

commit v2 on v1

--- a/solution.py
+++ b/solution.py
@@ -11,6 +11,7 @@
 STEPS = 3
 MESH = pl.DeviceIdType.MESH
 LOW = -1e30
+CODES = 32000.0
 
 
 def from_behind(array, axis, by):
@@ -79,10 +80,30 @@
     )
 
 
+def encode(dst, at, values):
+    wide = values.shape[1]
+    top = jnp.maximum(jnp.max(jnp.abs(values), axis=1, keepdims=True), 2.0**-110)
+    power = jnp.ceil(jnp.log2(top) * 64.0)
+    factor = jnp.exp2(power * (-1.0 / 64.0)) * CODES
+    dst[at, 0:wide] = jnp.round(values * factor).astype(jnp.int32).astype(jnp.int16)
+    dst[at, wide:] = (
+        jnp.broadcast_to(power, (values.shape[0], 128)).astype(jnp.int32).astype(jnp.int16)
+    )
+
+
+def decode(coded):
+    wide = coded.shape[1] - 128
+    power = coded[:, wide:].astype(jnp.int32).astype(jnp.float32)
+    factor = jnp.exp2(power * (1.0 / 64.0)) * (1.0 / CODES)
+    values = coded[:, 0:wide].astype(jnp.int32).astype(jnp.float32)
+    return values * jnp.concatenate([factor] * (wide // 128), axis=1)
+
+
 def kernel(
     scale, profile_scale,
-    ql_ref, tl_ref, q_hbm, t_hbm, prof_ref, sim_ref,
-    q_buf, t_buf, ql_buf, tl_buf, a_buf, r_buf, rx_a, rx_b, rx_c, rx_z, tx_s, rx_s,
+    ql_hbm, tl_hbm, q_hbm, t_hbm, prof_ref, sim_ref,
+    q_buf, t_buf, ql_buf, tl_buf, a_buf, r_buf, tx_a, tx_b, tx_c, tx_z, rx_a, rx_b, rx_c, rx_z,
+    tx_s, rx_s, ql_ref, tl_ref,
     local_sems, q_sems, l_sems, r_sems, z_sems, s_sems,
 ):
     res, wide = q_buf.shape[1:]
@@ -106,8 +127,14 @@
 
     load_q = pltpu.make_async_copy(q_hbm.at[c], q_buf.at[0], local_sems.at[0])
     load_t = pltpu.make_async_copy(t_hbm, t_buf.at[0], local_sems.at[1])
+    load_ql = pltpu.make_async_copy(ql_hbm, ql_ref, local_sems.at[2])
+    load_tl = pltpu.make_async_copy(tl_hbm, tl_ref, local_sems.at[3])
+    load_ql.start()
+    load_tl.start()
     load_q.start()
     load_t.start()
+    load_ql.wait()
+    load_tl.wait()
     ql_buf[0] = jnp.full((8, 128), ql_ref[c], jnp.int32)
     line = lax.broadcasted_iota(jnp.int32, (8, 128), 0)
     lengths = jnp.zeros((8, 128), jnp.int32)
@@ -215,7 +242,8 @@
     pass_on.start()
     send_len[0].wait_recv()
     both(1)
-    send_a = remote(r_buf.at[1], rx_a, r_sems, 0, (near, grp))
+    encode(tx_a, slice(None), r_buf[1])
+    send_a = remote(tx_a, rx_a, r_sems, 0, (near, grp))
     send_a.start()
     sims += send_sim(1)
 
@@ -239,8 +267,9 @@
 
     send_b, send_c, send_z = [], [], []
     for i in range(4):
+        encode(tx_b, rows(i), r_buf[3, rows(i), :])
         send_b.append(
-            remote(r_buf.at[3, rows(i)], rx_b.at[rows(i)], r_sems, 1 + i, (near, grp))
+            remote(tx_b.at[rows(i)], rx_b.at[rows(i)], r_sems, 1 + i, (near, grp))
         )
         send_b[i].start()
     sims += send_sim(3)
@@ -249,23 +278,26 @@
         if i == 0:
             send_a.wait_recv()
         send_c[i].wait_recv()
-        r_buf[0, rows(i), :] = r_buf[0, rows(i), :] + rx_a[rows(i), :] + rx_c[rows(i), :]
+        summed = r_buf[0, rows(i), :] + decode(rx_a[rows(i), :]) + decode(rx_c[rows(i), :])
+        encode(tx_z, rows(i), summed)
+        if i == 3:
+            r_buf[0, rows(i), :] = summed
         for u in range(2):
             core = 1 - c if u else c
             there = chunk(i) * 2 + core
             if i < 3 or u:
                 mine = pl.ds(pl.multiple_of(there * half, half), half)
                 copy = remote(
-                    r_buf.at[0, mine], rx_z.at[i, u], z_sems, i * 2 + u, (blk, there)
+                    tx_z.at[mine], rx_z.at[i, u], z_sems, i * 2 + u, (blk, there)
                 )
                 copy.start()
                 send_z.append(copy)
 
     for i in range(4):
         send_b[i].wait_recv()
-        r_buf[2, rows(i), :] = r_buf[2, rows(i), :] + rx_b[rows(i), :]
+        encode(tx_c, rows(i), r_buf[2, rows(i), :] + decode(rx_b[rows(i), :]))
         send_c.append(
-            remote(r_buf.at[2, rows(i)], rx_c.at[rows(i)], r_sems, 5 + i, (far, grp))
+            remote(tx_c.at[rows(i)], rx_c.at[rows(i)], r_sems, 5 + i, (far, grp))
         )
         send_c[i].start()
         if i:
@@ -285,10 +317,10 @@
         copy.wait_recv()
     own = pl.ds(pl.multiple_of(grp * half, half), half)
     prof_ref[c] = (
-        r_buf[0, own, :] + rx_z[0, 0] + rx_z[1, 0] + rx_z[2, 0]
+        r_buf[0, own, :] + decode(rx_z[0, 0]) + decode(rx_z[1, 0]) + decode(rx_z[2, 0])
     ) * profile_scale
     prof_ref[1 - c] = (
-        rx_z[0, 1] + rx_z[1, 1] + rx_z[2, 1] + rx_z[3, 1]
+        decode(rx_z[0, 1]) + decode(rx_z[1, 1]) + decode(rx_z[2, 1]) + decode(rx_z[3, 1])
     ) * profile_scale
 
     for copy in (
@@ -312,8 +344,8 @@
             jax.ShapeDtypeStruct((sets, (STEPS + 1) * per_core), f32),
         ),
         in_specs=[
-            pl.BlockSpec(memory_space=pltpu.SMEM),
-            pl.BlockSpec(memory_space=pltpu.SMEM),
+            pl.BlockSpec(memory_space=pl.ANY),
+            pl.BlockSpec(memory_space=pl.ANY),
             pl.BlockSpec(memory_space=pl.ANY),
             pl.BlockSpec(memory_space=pl.ANY),
         ],
@@ -325,13 +357,13 @@
             vmem((2, 8, 128), jnp.int32),
             vmem((2, res, per_core * res), bf16),
             vmem((4, res, wide), f32),
-            vmem((res, wide), f32),
-            vmem((res, wide), f32),
-            vmem((res, wide), f32),
-            vmem((4, 2, part, wide), f32),
+            *[vmem((res, wide + 128), jnp.int16) for _ in range(7)],
+            vmem((4, 2, part, wide + 128), jnp.int16),
             vmem((4, 2, 8, 128), f32),
             vmem((4, 2, 8, 128), f32),
-            pltpu.SemaphoreType.DMA((2,)),
+            pltpu.SMEM(query_lengths.shape, jnp.int32),
+            pltpu.SMEM(target_lengths.shape, jnp.int32),
+            pltpu.SemaphoreType.DMA((4,)),
             pltpu.SemaphoreType.DMA((2, 4)),
             pltpu.SemaphoreType.DMA((2, 4)),
             pltpu.SemaphoreType.DMA((2, 9)),
@@ -339,7 +371,7 @@
             pltpu.SemaphoreType.DMA((2, 8)),
         ],
         compiler_params=pltpu.CompilerParams(
-            collective_id=0, has_side_effects=True, vmem_limit_bytes=40 * 1024 * 1024
+            collective_id=0, has_side_effects=True, vmem_limit_bytes=60 * 1024 * 1024
         ),
     )(query_lengths, target_lengths, queries, targets)
 

time: 56.7 us -> 45.4 us (0.80)
  the two profiles are of different devices: /device:TPU:9 before, /device:TPU:0 now
where the time goes in v2:
time: 45.4 us; the launch traced here: 44.8 us
  Pallas kernels  41.4 us (91%)
  local copies, waits for them, and re-layouts  2.79 us (6%)
  between operations  0.64 us (1%)
    pallas_call x1, Pallas kernels, plane_shards(): pl.pallas_call(functools.partial(kernel, scale, profile_scale), out_shape...  41.4 us
    unnamed x2, local copies, waits for them, and re-layouts  2.79 us

profile of v2, /device:TPU:0, one launch (start us, length us, event | category | flops | bytes accessed | tf_op | source)
XLA Modules:
  0.0 44.8 jit_solution(4852081319592188346)
XLA Ops:
  0.6 41.4 %shard_map.59 = (f32[2,16,1280]{2,1,0:T(8,128)}, f32[2,16]{1,0:T(2,128)}) custom-call(s32[2]{0:T(128)} %ql_hbm.1, s32[4]{0:T(128)} %tl_hbm.1, bf16[2,128,1280]{2,1,0:T(8,128)(2,1)} %q_hbm.1, bf16[4,128,1280]{2,1,0:T(8,128)(2,1)} %t_hbm.1), custom_call_target="tpu_custom_call" | custom-call | tf_op jit(solution)/shard_map/pallas_call | solution.py:340
  42.0 1.6 %copy.8 = f32[2,16,1280]{2,1,0:T(8,128)} copy(f32[2,16,1280]{2,1,0:T(8,128)} %get-tuple-element.4) | data formatting | bytes 327680
  43.6 1.2 %copy.9 = f32[2,16]{1,0:T(2,128)} copy(f32[2,16]{1,0:T(2,128)} %get-tuple-element.5) | data formatting | bytes 256

commit v3 on v2

--- a/solution.py
+++ b/solution.py
@@ -102,7 +102,7 @@
 def kernel(
     scale, profile_scale,
     ql_hbm, tl_hbm, q_hbm, t_hbm, prof_ref, sim_ref,
-    q_buf, t_buf, ql_buf, tl_buf, a_buf, r_buf, tx_a, tx_b, tx_c, tx_z, rx_a, rx_b, rx_c, rx_z,
+    q_buf, t_buf, ql_buf, tl_buf, s_buf, w_buf, a_buf, r_buf, tx_a, tx_b, tx_c, tx_z, rx_a, rx_b, rx_c, rx_z,
     tx_s, rx_s, ql_ref, tl_ref,
     local_sems, q_sems, l_sems, r_sems, z_sems, s_sems,
 ):
@@ -143,12 +143,20 @@
     tl_buf[0] = lengths
     pl.semaphore_wait(barrier, len(partners))
 
-    send_near = remote(q_hbm.at[c], q_buf.at[1], q_sems, 0, (near, grp))
-    send_far = remote(q_hbm.at[c], q_buf.at[2], q_sems, 1, (far, grp))
-    send_t = remote(t_hbm, t_buf.at[1], q_sems, 3, (blk, sibling))
-    pass_on = remote(q_buf.at[1], q_buf.at[3], q_sems, 2, (far, grp))
-    send_near.start()
-    send_far.start()
+    split = res // 2
+    halves = [pl.ds(0, split), pl.ds(split, split)]
+    send_near = [
+        remote(q_hbm.at[c, part], q_buf.at[1, part], q_sems, n, (near, grp))
+        for n, part in enumerate(halves)
+    ]
+    pass_on = [
+        remote(q_buf.at[1, part], q_buf.at[3, part], q_sems, 2 + n, (far, grp))
+        for n, part in enumerate(halves)
+    ]
+    send_far = remote(q_hbm.at[c], q_buf.at[2], q_sems, 4, (far, grp))
+    send_t = remote(t_hbm, t_buf.at[1], q_sems, 5, (blk, sibling))
+    for copy in send_near:
+        copy.start()
     send_t.start()
     send_len = [
         remote(ql_buf.at[0], ql_buf.at[s], l_sems, s - 1, (blks[s], grp)) for s in range(1, 4)
@@ -168,21 +176,32 @@
             (((1,), (1,)), ((), ())),
             preferred_element_type=jnp.float32,
         ) * scale
+        row_ok_vec = (row_at < ql_buf[s, 0:1, :])[:, 0:1]
+        for r in range(per_core):
+            cols = slice(r * res, (r + 1) * res)
+            scores = scores_all[:, cols]
+            s_buf[s, h, :, cols] = scores
+            by_row = jnp.where(col_at < tl_buf[h, r : r + 1, :], scores, LOW)
+            row_exp = jnp.exp(by_row - jnp.max(by_row, axis=1, keepdims=True))
+            row_inv = jnp.where(row_ok_vec, 1.0 / jnp.sum(row_exp, axis=1, keepdims=True), 0.0)
+            row_soft = row_exp * row_inv
+            w_buf[s, h, :, cols] = row_soft
+            a_buf[h, :, cols] = row_soft.astype(jnp.bfloat16)
+
+    def similar(s, h):
         row_ok = row_at < ql_buf[s, 0:1, :]
-        row_ok_vec = row_ok[:, 0:1]
         place = ((blks[s] - blk + 4) % 4) * per_core
         tile = jnp.zeros((8, 128), jnp.float32)
         for r in range(per_core):
-            scores = scores_all[:, r * res : (r + 1) * res]
-            col_ok = col_at < tl_buf[h, r : r + 1, :]
-            by_row = jnp.where(col_ok, scores, LOW)
-            row_exp = jnp.exp(by_row - jnp.max(by_row, axis=1, keepdims=True))
-            row_inv = jnp.where(row_ok_vec, 1.0 / jnp.sum(row_exp, axis=1, keepdims=True), 0.0)
-            row_soft = row_exp * row_inv
+            cols = slice(r * res, (r + 1) * res)
+            scores = s_buf[s, h, :, cols]
+            row_soft = w_buf[s, h, :, cols]
             by_col = jnp.where(row_ok, scores, LOW)
             col_exp = jnp.exp(by_col - jnp.max(by_col, axis=0, keepdims=True))
             col_inv = jnp.where(
-                col_ok[0:1, :], 1.0 / jnp.sum(col_exp, axis=0, keepdims=True), 0.0
+                col_at[0:1, :] < tl_buf[h, r : r + 1, :],
+                1.0 / jnp.sum(col_exp, axis=0, keepdims=True),
+                0.0,
             )
             col_soft = col_exp * col_inv
             weights = row_soft + col_soft - row_soft * col_soft
@@ -191,7 +210,6 @@
             )
             lower = jnp.sum(jnp.sum(weights, axis=0, keepdims=True), axis=1, keepdims=True)
             tile = jnp.where((line == c) & (lane == place + r), upper / lower, tile)
-            a_buf[h, :, r * res : (r + 1) * res] = row_soft.astype(jnp.bfloat16)
         tx_s[s, h] = tile
 
     def profile(s):
@@ -219,7 +237,12 @@
         lax.fori_loop(0, 2, body, 0)
         profile(s)
 
-    def send_sim(s):
+    def similarities(s):
+        def body(h, carry):
+            similar(s, h)
+            return carry
+
+        lax.fori_loop(0, 2, body, 0)
         out = []
         for h in range(2):
             if s or h:
@@ -233,26 +256,24 @@
 
     load_q.wait()
     load_t.wait()
+    align(0, 0)
+    for n in range(2):
+        send_near[n].wait_recv()
+        pass_on[n].start()
+    send_far.start()
     send_t.wait_recv()
     send_len[3].wait_recv()
-    both(0)
-    sims = send_sim(0)
-
-    send_near.wait_recv()
-    pass_on.start()
+    align(0, 1)
+    profile(0)
+
     send_len[0].wait_recv()
     both(1)
     encode(tx_a, slice(None), r_buf[1])
     send_a = remote(tx_a, rx_a, r_sems, 0, (near, grp))
     send_a.start()
-    sims += send_sim(1)
-
-    send_far.wait_recv()
-    send_len[1].wait_recv()
-    both(2)
-    sims += send_sim(2)
-
-    pass_on.wait_recv()
+
+    for n in range(2):
+        pass_on[n].wait_recv()
     send_len[2].wait_recv()
     both(3)
 
@@ -272,7 +293,10 @@
             remote(tx_b.at[rows(i)], rx_b.at[rows(i)], r_sems, 1 + i, (near, grp))
         )
         send_b[i].start()
-    sims += send_sim(3)
+
+    send_far.wait_recv()
+    send_len[1].wait_recv()
+    both(2)
 
     def finish(i):
         if i == 0:
@@ -300,9 +324,12 @@
             remote(tx_c.at[rows(i)], rx_c.at[rows(i)], r_sems, 5 + i, (far, grp))
         )
         send_c[i].start()
-        if i:
-            finish(i - 1)
-    finish(3)
+    sims = similarities(0)
+    sims += similarities(1)
+    for i in range(4):
+        finish(i)
+    sims += similarities(2)
+    sims += similarities(3)
 
     total = tx_s[0, 0]
     for copy in sims:
@@ -324,7 +351,8 @@
     ) * profile_scale
 
     for copy in (
-        [send_near, send_far, send_t, pass_on, send_a] + send_len + sims + send_b + send_c + send_z
+        send_near + pass_on + [send_far, send_t, send_a]
+        + send_len + sims + send_b + send_c + send_z
     ):
         copy.wait_send()
 
@@ -344,10 +372,10 @@
             jax.ShapeDtypeStruct((sets, (STEPS + 1) * per_core), f32),
         ),
         in_specs=[
-            pl.BlockSpec(memory_space=pl.ANY),
-            pl.BlockSpec(memory_space=pl.ANY),
-            pl.BlockSpec(memory_space=pl.ANY),
-            pl.BlockSpec(memory_space=pl.ANY),
+            pl.BlockSpec(memory_space=pltpu.HBM),
+            pl.BlockSpec(memory_space=pltpu.HBM),
+            pl.BlockSpec(memory_space=pltpu.HBM),
+            pl.BlockSpec(memory_space=pltpu.HBM),
         ],
         out_specs=(pl.BlockSpec(memory_space=vmem), pl.BlockSpec(memory_space=vmem)),
         scratch_shapes=[
@@ -355,6 +383,8 @@
             vmem((2, per_core, res, wide), bf16),
             vmem((4, 8, 128), jnp.int32),
             vmem((2, 8, 128), jnp.int32),
+            vmem((4, 2, res, per_core * res), f32),
+            vmem((4, 2, res, per_core * res), f32),
             vmem((2, res, per_core * res), bf16),
             vmem((4, res, wide), f32),
             *[vmem((res, wide + 128), jnp.int16) for _ in range(7)],
@@ -364,14 +394,14 @@
             pltpu.SMEM(query_lengths.shape, jnp.int32),
             pltpu.SMEM(target_lengths.shape, jnp.int32),
             pltpu.SemaphoreType.DMA((4,)),
-            pltpu.SemaphoreType.DMA((2, 4)),
+            pltpu.SemaphoreType.DMA((2, 6)),
             pltpu.SemaphoreType.DMA((2, 4)),
             pltpu.SemaphoreType.DMA((2, 9)),
             pltpu.SemaphoreType.DMA((2, 8)),
             pltpu.SemaphoreType.DMA((2, 8)),
         ],
         compiler_params=pltpu.CompilerParams(
-            collective_id=0, has_side_effects=True, vmem_limit_bytes=60 * 1024 * 1024
+            collective_id=0, has_side_effects=True, vmem_limit_bytes=56 * 1024 * 1024
         ),
     )(query_lengths, target_lengths, queries, targets)
 

time: 45.4 us -> 42.9 us (0.945)
  Pallas kernels: 41.4 us -> 39.3 us
    pallas_call x1, Pallas kernels: 41.4 us -> 39.3 us  [plane_shards(): pl.pallas_call(functools.partial(kernel, scale, profile_scale), out_shape...]
where the time goes in v3:
time: 42.9 us; the launch traced here: 42.7 us
  Pallas kernels  39.3 us (92%)
  local copies, waits for them, and re-layouts  2.79 us (7%)
  between operations  0.64 us (1%)
    pallas_call x1, Pallas kernels, plane_shards(): pl.pallas_call(functools.partial(kernel, scale, profile_scale), out_shape...  39.3 us
    unnamed x2, local copies, waits for them, and re-layouts  2.79 us

profile of v3, /device:TPU:0, one launch (start us, length us, event | category | flops | bytes accessed | tf_op | source)
XLA Modules:
  0.0 42.7 jit_solution(16945554372041689638)
XLA Ops:
  0.6 39.3 %shard_map.59 = (f32[2,16,1280]{2,1,0:T(8,128)}, f32[2,16]{1,0:T(2,128)}) custom-call(s32[2]{0:T(128)} %ql_hbm.1, s32[4]{0:T(128)} %tl_hbm.1, bf16[2,128,1280]{2,1,0:T(8,128)(2,1)} %q_hbm.1, bf16[4,128,1280]{2,1,0:T(8,128)(2,1)} %t_hbm.1), custom_call_target="tpu_custom_call" | custom-call | tf_op jit(solution)/shard_map/pallas_call | solution.py:368
  39.9 1.6 %copy.8 = f32[2,16,1280]{2,1,0:T(8,128)} copy(f32[2,16,1280]{2,1,0:T(8,128)} %get-tuple-element.4) | data formatting | bytes 327680
  41.5 1.2 %copy.9 = f32[2,16]{1,0:T(2,128)} copy(f32[2,16]{1,0:T(2,128)} %get-tuple-element.5) | data formatting | bytes 256

commit v4 on v3

--- a/solution.py
+++ b/solution.py
@@ -169,24 +169,26 @@
     col_at = lax.broadcasted_iota(jnp.int32, (res, res), 1)
     row_at = lax.broadcasted_iota(jnp.int32, (res, res), 0)
 
-    def align(s, h):
+    def align(s, first, last):
         scores_all = lax.dot_general(
             q_buf[s],
-            t_buf[h].reshape(per_core * res, wide),
+            t_buf[first:last].reshape((last - first) * per_core * res, wide),
             (((1,), (1,)), ((), ())),
             preferred_element_type=jnp.float32,
         ) * scale
         row_ok_vec = (row_at < ql_buf[s, 0:1, :])[:, 0:1]
-        for r in range(per_core):
+        for h, r in [(h, r) for h in range(first, last) for r in range(per_core)]:
             cols = slice(r * res, (r + 1) * res)
-            scores = scores_all[:, cols]
+            at = ((h - first) * per_core + r) * res
+            scores = scores_all[:, at : at + res]
             s_buf[s, h, :, cols] = scores
             by_row = jnp.where(col_at < tl_buf[h, r : r + 1, :], scores, LOW)
             row_exp = jnp.exp(by_row - jnp.max(by_row, axis=1, keepdims=True))
             row_inv = jnp.where(row_ok_vec, 1.0 / jnp.sum(row_exp, axis=1, keepdims=True), 0.0)
             row_soft = row_exp * row_inv
             w_buf[s, h, :, cols] = row_soft
-            a_buf[h, :, cols] = row_soft.astype(jnp.bfloat16)
+            at = (h * per_core + r) * res
+            a_buf[:, at : at + res] = row_soft.astype(jnp.bfloat16)
 
     def similar(s, h):
         row_ok = row_at < ql_buf[s, 0:1, :]
@@ -213,28 +215,14 @@
         tx_s[s, h] = tile
 
     def profile(s):
-        step = 256
-
-        def body(n, carry):
-            cols = pl.ds(pl.multiple_of(n * step, step), step)
-            r_buf[s, :, cols] = sum(
-                jnp.dot(
-                    a_buf[h],
-                    t_buf[h, :, :, cols].reshape(per_core * res, step),
-                    preferred_element_type=jnp.float32,
-                )
-                for h in range(2)
-            )
-            return carry
-
-        lax.fori_loop(0, wide // step, body, 0)
+        r_buf[s] = jnp.dot(
+            a_buf[...],
+            t_buf[...].reshape(2 * per_core * res, wide),
+            preferred_element_type=jnp.float32,
+        )
 
     def both(s):
-        def body(h, carry):
-            align(s, h)
-            return carry
-
-        lax.fori_loop(0, 2, body, 0)
+        align(s, 0, 2)
         profile(s)
 
     def similarities(s):
@@ -256,15 +244,15 @@
 
     load_q.wait()
     load_t.wait()
-    align(0, 0)
+    align(0, 0, 1)
     for n in range(2):
         send_near[n].wait_recv()
         pass_on[n].start()
-    send_far.start()
     send_t.wait_recv()
     send_len[3].wait_recv()
-    align(0, 1)
+    align(0, 1, 2)
     profile(0)
+    send_far.start()
 
     send_len[0].wait_recv()
     both(1)
@@ -325,9 +313,9 @@
         )
         send_c[i].start()
     sims = similarities(0)
-    sims += similarities(1)
     for i in range(4):
         finish(i)
+    sims += similarities(1)
     sims += similarities(2)
     sims += similarities(3)
 
@@ -385,7 +373,7 @@
             vmem((2, 8, 128), jnp.int32),
             vmem((4, 2, res, per_core * res), f32),
             vmem((4, 2, res, per_core * res), f32),
-            vmem((2, res, per_core * res), bf16),
+            vmem((res, 2 * per_core * res), bf16),
             vmem((4, res, wide), f32),
             *[vmem((res, wide + 128), jnp.int16) for _ in range(7)],
             vmem((4, 2, part, wide + 128), jnp.int16),

time: 42.9 us -> 43 us (level)
  no operation moved by 1% of the time
where the time goes in v4:
time: 43 us; the launch traced here: 42.8 us
  Pallas kernels  39.4 us (92%)
  local copies, waits for them, and re-layouts  2.79 us (6%)
  between operations  0.64 us (1%)
    pallas_call x1, Pallas kernels, plane_shards(): pl.pallas_call(functools.partial(kernel, scale, profile_scale), out_shape...  39.4 us
    unnamed x2, local copies, waits for them, and re-layouts  2.79 us

profile of v4, /device:TPU:0, one launch (start us, length us, event | category | flops | bytes accessed | tf_op | source)
XLA Modules:
  0.0 42.8 jit_solution(13616930376687547440)
XLA Ops:
  0.6 39.4 %shard_map.59 = (f32[2,16,1280]{2,1,0:T(8,128)}, f32[2,16]{1,0:T(2,128)}) custom-call(s32[2]{0:T(128)} %ql_hbm.1, s32[4]{0:T(128)} %tl_hbm.1, bf16[2,128,1280]{2,1,0:T(8,128)(2,1)} %q_hbm.1, bf16[4,128,1280]{2,1,0:T(8,128)(2,1)} %t_hbm.1), custom_call_target="tpu_custom_call" | custom-call | tf_op jit(solution)/shard_map/pallas_call | solution.py:356
  40.0 1.6 %copy.8 = f32[2,16,1280]{2,1,0:T(8,128)} copy(f32[2,16,1280]{2,1,0:T(8,128)} %get-tuple-element.4) | data formatting | bytes 327680
  41.6 1.2 %copy.9 = f32[2,16]{1,0:T(2,128)} copy(f32[2,16]{1,0:T(2,128)} %get-tuple-element.5) | data formatting | bytes 256

commit v5 on v3

--- a/solution.py
+++ b/solution.py
@@ -102,7 +102,7 @@
 def kernel(
     scale, profile_scale,
     ql_hbm, tl_hbm, q_hbm, t_hbm, prof_ref, sim_ref,
-    q_buf, t_buf, ql_buf, tl_buf, s_buf, w_buf, a_buf, r_buf, tx_a, tx_b, tx_c, tx_z, rx_a, rx_b, rx_c, rx_z,
+    q_buf, t_buf, ql_buf, tl_buf, s_buf, w_buf, a_buf, r_buf, tx, rx, rx_z,
     tx_s, rx_s, ql_ref, tl_ref,
     local_sems, q_sems, l_sems, r_sems, z_sems, s_sems,
 ):
@@ -114,7 +114,7 @@
     other_x, other_y = y * 2 + (1 - x), (1 - y) * 2 + x
     near = other_x * (1 - c) + other_y * c
     far = other_y * (1 - c) + other_x * c
-    blks = (blk, near, far, 3 - blk)
+    blks = (blk, near, 3 - blk, far)
     sibling = z * 2 + (1 - c)
 
     barrier = pltpu.get_barrier_semaphore()
@@ -150,10 +150,10 @@
         for n, part in enumerate(halves)
     ]
     pass_on = [
-        remote(q_buf.at[1, part], q_buf.at[3, part], q_sems, 2 + n, (far, grp))
+        remote(q_buf.at[1, part], q_buf.at[2, part], q_sems, 2 + n, (far, grp))
         for n, part in enumerate(halves)
     ]
-    send_far = remote(q_hbm.at[c], q_buf.at[2], q_sems, 4, (far, grp))
+    send_far = remote(q_hbm.at[c], q_buf.at[3], q_sems, 4, (far, grp))
     send_t = remote(t_hbm, t_buf.at[1], q_sems, 5, (blk, sibling))
     for copy in send_near:
         copy.start()
@@ -168,6 +168,25 @@
     lane = lax.broadcasted_iota(jnp.int32, (8, 128), 1)
     col_at = lax.broadcasted_iota(jnp.int32, (res, res), 1)
     row_at = lax.broadcasted_iota(jnp.int32, (res, res), 0)
+    quarter = res // 4
+    half = quarter // 2
+
+    def chunk(i):
+        return (z + 1 + i) % 4
+
+    def rows(i):
+        return pl.ds(pl.multiple_of(chunk(i) * quarter, quarter), quarter)
+
+    def sum_copy(s, i):
+        return remote(tx.at[s, rows(i)], rx.at[s, rows(i)], r_sems, s * 4 + i, (near, grp))
+
+    def far_copy(i):
+        return remote(tx.at[2, rows(i)], rx.at[2, rows(i)], r_sems, 8 + i, (far, grp))
+
+    def z_copy(i, u):
+        there = chunk(i) * 2 + (1 - c if u else c)
+        mine = pl.ds(pl.multiple_of(there * half, half), half)
+        return remote(tx.at[3, mine], rx_z.at[i, u], z_sems, i * 2 + u, (blk, there))
 
     def align(s, h):
         scores_all = lax.dot_general(
@@ -188,9 +207,25 @@
             w_buf[s, h, :, cols] = row_soft
             a_buf[h, :, cols] = row_soft.astype(jnp.bfloat16)
 
+    def profile(s):
+        r_buf[s] = sum(
+            jnp.dot(
+                a_buf[h],
+                t_buf[h].reshape(per_core * res, wide),
+                preferred_element_type=jnp.float32,
+            )
+            for h in range(2)
+        )
+
     def similar(s, h):
         row_ok = row_at < ql_buf[s, 0:1, :]
-        place = ((blks[s] - blk + 4) % 4) * per_core
+        peer = (
+            blk
+            + (s * (3 - s) * (2 - s) // 2) * (near - blk)
+            + (s * (3 - s) * (s - 1) // 2) * (3 - 2 * blk)
+            + (s * (s - 1) * (s - 2) // 6) * (far - blk)
+        )
+        place = ((peer - blk + 4) % 4) * per_core
         tile = jnp.zeros((8, 128), jnp.float32)
         for r in range(per_core):
             cols = slice(r * res, (r + 1) * res)
@@ -199,7 +234,7 @@
             by_col = jnp.where(row_ok, scores, LOW)
             col_exp = jnp.exp(by_col - jnp.max(by_col, axis=0, keepdims=True))
             col_inv = jnp.where(
-                col_at[0:1, :] < tl_buf[h, r : r + 1, :],
+                col_at[0:1, :] < tl_buf[h, pl.ds(r, 1), :],
                 1.0 / jnp.sum(col_exp, axis=0, keepdims=True),
                 0.0,
             )
@@ -212,124 +247,93 @@
             tile = jnp.where((line == c) & (lane == place + r), upper / lower, tile)
         tx_s[s, h] = tile
 
-    def profile(s):
-        step = 256
-
-        def body(n, carry):
-            cols = pl.ds(pl.multiple_of(n * step, step), step)
-            r_buf[s, :, cols] = sum(
-                jnp.dot(
-                    a_buf[h],
-                    t_buf[h, :, :, cols].reshape(per_core * res, step),
-                    preferred_element_type=jnp.float32,
-                )
-                for h in range(2)
-            )
-            return carry
-
-        lax.fori_loop(0, wide // step, body, 0)
-
-    def both(s):
-        def body(h, carry):
-            align(s, h)
-            return carry
-
-        lax.fori_loop(0, 2, body, 0)
-        profile(s)
-
-    def similarities(s):
-        def body(h, carry):
-            similar(s, h)
-            return carry
-
-        lax.fori_loop(0, 2, body, 0)
-        out = []
-        for h in range(2):
-            if s or h:
-                copy = remote(
-                    tx_s.at[s, h], rx_s.at[s, h], s_sems, s * 2 + h,
-                    (blks[s], sibling if h else grp),
-                )
-                copy.start()
-                out.append(copy)
-        return out
-
     load_q.wait()
     load_t.wait()
-    align(0, 0)
-    for n in range(2):
-        send_near[n].wait_recv()
-        pass_on[n].start()
-    send_far.start()
-    send_t.wait_recv()
-    send_len[3].wait_recv()
-    align(0, 1)
-    profile(0)
-
-    send_len[0].wait_recv()
-    both(1)
-    encode(tx_a, slice(None), r_buf[1])
-    send_a = remote(tx_a, rx_a, r_sems, 0, (near, grp))
-    send_a.start()
-
-    for n in range(2):
-        pass_on[n].wait_recv()
-    send_len[2].wait_recv()
-    both(3)
-
-    quarter = res // 4
-    half = quarter // 2
-
-    def chunk(i):
-        return (z + 1 + i) % 4
-
-    def rows(i):
-        return pl.ds(pl.multiple_of(chunk(i) * quarter, quarter), quarter)
-
-    send_b, send_c, send_z = [], [], []
+
+    @pl.loop(0, 8)
+    def _(n):
+        s, h = n // 2, n % 2
+
+        @pl.when(n == 1)
+        def _():
+            for m in range(2):
+                send_near[m].wait_recv()
+                pass_on[m].start()
+            send_t.wait_recv()
+            send_len[3].wait_recv()
+
+        @pl.when(n == 2)
+        def _():
+            send_far.start()
+            send_len[0].wait_recv()
+
+        @pl.when(n == 4)
+        def _():
+            for m in range(2):
+                pass_on[m].wait_recv()
+            send_len[1].wait_recv()
+
+        @pl.when(n == 6)
+        def _():
+            send_far.wait_recv()
+            send_len[2].wait_recv()
+
+        align(s, h)
+
+        @pl.when(h == 1)
+        def _():
+            profile(s)
+
+        @pl.when((n == 3) | (n == 5))
+        def _():
+            @pl.loop(0, 4)
+            def _(i):
+                encode(tx.at[s - 1], rows(i), r_buf[s, rows(i), :])
+                sum_copy(s - 1, i).start()
+
+    @pl.loop(0, 4)
+    def _(i):
+        sum_copy(1, i).wait_recv()
+        encode(tx.at[2], rows(i), r_buf[3, rows(i), :] + decode(rx[1, rows(i), :]))
+        far_copy(i).start()
+
+    @pl.loop(0, 4)
+    def _(i):
+        sum_copy(0, i).wait_recv()
+        far_copy(i).wait_recv()
+        summed = r_buf[0, rows(i), :] + decode(rx[0, rows(i), :]) + decode(rx[2, rows(i), :])
+        r_buf[0, rows(i), :] = summed
+        encode(tx.at[3], rows(i), summed)
+        z_copy(i, 1).start()
+
+        @pl.when(i < 3)
+        def _():
+            z_copy(i, 0).start()
+
+    @pl.loop(0, 8)
+    def _(n):
+        similar(n // 2, n % 2)
+
+    sims = [
+        remote(
+            tx_s.at[s, h], rx_s.at[s, h], s_sems, s * 2 + h, (blks[s], sibling if h else grp)
+        )
+        for s in range(4) for h in range(2) if s or h
+    ]
+    for copy in sims:
+        copy.start()
+
+    own = pl.ds(pl.multiple_of(grp * half, half), half)
+    here, there = r_buf[0, own, :], None
     for i in range(4):
-        encode(tx_b, rows(i), r_buf[3, rows(i), :])
-        send_b.append(
-            remote(tx_b.at[rows(i)], rx_b.at[rows(i)], r_sems, 1 + i, (near, grp))
-        )
-        send_b[i].start()
-
-    send_far.wait_recv()
-    send_len[1].wait_recv()
-    both(2)
-
-    def finish(i):
-        if i == 0:
-            send_a.wait_recv()
-        send_c[i].wait_recv()
-        summed = r_buf[0, rows(i), :] + decode(rx_a[rows(i), :]) + decode(rx_c[rows(i), :])
-        encode(tx_z, rows(i), summed)
-        if i == 3:
-            r_buf[0, rows(i), :] = summed
-        for u in range(2):
-            core = 1 - c if u else c
-            there = chunk(i) * 2 + core
-            if i < 3 or u:
-                mine = pl.ds(pl.multiple_of(there * half, half), half)
-                copy = remote(
-                    tx_z.at[mine], rx_z.at[i, u], z_sems, i * 2 + u, (blk, there)
-                )
-                copy.start()
-                send_z.append(copy)
-
-    for i in range(4):
-        send_b[i].wait_recv()
-        encode(tx_c, rows(i), r_buf[2, rows(i), :] + decode(rx_b[rows(i), :]))
-        send_c.append(
-            remote(tx_c.at[rows(i)], rx_c.at[rows(i)], r_sems, 5 + i, (far, grp))
-        )
-        send_c[i].start()
-    sims = similarities(0)
-    sims += similarities(1)
-    for i in range(4):
-        finish(i)
-    sims += similarities(2)
-    sims += similarities(3)
+        z_copy(i, 1).wait_recv()
+        part = decode(rx_z[i, 1])
+        there = part if there is None else there + part
+        if i < 3:
+            z_copy(i, 0).wait_recv()
+            here = here + decode(rx_z[i, 0])
+    prof_ref[c] = here * profile_scale
+    prof_ref[1 - c] = there * profile_scale
 
     total = tx_s[0, 0]
     for copy in sims:
@@ -340,21 +344,15 @@
                 total = total + rx_s[s, h]
     sim_ref[...] = total[0:2, 0 : sim_ref.shape[1]]
 
-    for copy in send_z:
-        copy.wait_recv()
-    own = pl.ds(pl.multiple_of(grp * half, half), half)
-    prof_ref[c] = (
-        r_buf[0, own, :] + decode(rx_z[0, 0]) + decode(rx_z[1, 0]) + decode(rx_z[2, 0])
-    ) * profile_scale
-    prof_ref[1 - c] = (
-        decode(rx_z[0, 1]) + decode(rx_z[1, 1]) + decode(rx_z[2, 1]) + decode(rx_z[3, 1])
-    ) * profile_scale
-
-    for copy in (
-        send_near + pass_on + [send_far, send_t, send_a]
-        + send_len + sims + send_b + send_c + send_z
-    ):
+    for copy in send_near + pass_on + [send_far, send_t] + send_len + sims:
         copy.wait_send()
+    for i in range(4):
+        sum_copy(0, i).wait_send()
+        sum_copy(1, i).wait_send()
+        far_copy(i).wait_send()
+        z_copy(i, 1).wait_send()
+        if i < 3:
+            z_copy(i, 0).wait_send()
 
 
 def plane_shards(queries, query_lengths, targets, target_lengths):
@@ -387,7 +385,8 @@
             vmem((4, 2, res, per_core * res), f32),
             vmem((2, res, per_core * res), bf16),
             vmem((4, res, wide), f32),
-            *[vmem((res, wide + 128), jnp.int16) for _ in range(7)],
+            vmem((4, res, wide + 128), jnp.int16),
+            vmem((3, res, wide + 128), jnp.int16),
             vmem((4, 2, part, wide + 128), jnp.int16),
             vmem((4, 2, 8, 128), f32),
             vmem((4, 2, 8, 128), f32),
@@ -396,7 +395,7 @@
             pltpu.SemaphoreType.DMA((4,)),
             pltpu.SemaphoreType.DMA((2, 6)),
             pltpu.SemaphoreType.DMA((2, 4)),
-            pltpu.SemaphoreType.DMA((2, 9)),
+            pltpu.SemaphoreType.DMA((2, 12)),
             pltpu.SemaphoreType.DMA((2, 8)),
             pltpu.SemaphoreType.DMA((2, 8)),
         ],

time: 42.9 us -> 43.7 us (1.019)
  Pallas kernels: 39.3 us -> 40.1 us
    pallas_call x1, Pallas kernels: 39.3 us -> 40.1 us  [plane_shards(): pl.pallas_call(functools.partial(kernel, scale, profile_scale), out_shape...]
where the time goes in v5:
time: 43.7 us; the launch traced here: 43.5 us
  Pallas kernels  40.1 us (92%)
  local copies, waits for them, and re-layouts  2.79 us (6%)
  between operations  0.64 us (1%)
    pallas_call x1, Pallas kernels, plane_shards(): pl.pallas_call(functools.partial(kernel, scale, profile_scale), out_shape...  40.1 us
    unnamed x2, local copies, waits for them, and re-layouts  2.79 us

profile of v5, /device:TPU:0, one launch (start us, length us, event | category | flops | bytes accessed | tf_op | source)
XLA Modules:
  0.0 43.5 jit_solution(17390173294798970307)
XLA Ops:
  0.6 40.1 %shard_map.59 = (f32[2,16,1280]{2,1,0:T(8,128)}, f32[2,16]{1,0:T(2,128)}) custom-call(s32[2]{0:T(128)} %ql_hbm.1, s32[4]{0:T(128)} %tl_hbm.1, bf16[2,128,1280]{2,1,0:T(8,128)(2,1)} %q_hbm.1, bf16[4,128,1280]{2,1,0:T(8,128)(2,1)} %t_hbm.1), custom_call_target="tpu_custom_call" | custom-call | tf_op jit(solution)/shard_map/pallas_call | solution.py:366
  40.7 1.6 %copy.8 = f32[2,16,1280]{2,1,0:T(8,128)} copy(f32[2,16,1280]{2,1,0:T(8,128)} %get-tuple-element.4) | data formatting | bytes 327680
  42.3 1.2 %copy.9 = f32[2,16]{1,0:T(2,128)} copy(f32[2,16]{1,0:T(2,128)} %get-tuple-element.5) | data formatting | bytes 256

commit v6 on v4

--- a/solution.py
+++ b/solution.py
@@ -312,9 +312,9 @@
             remote(tx_c.at[rows(i)], rx_c.at[rows(i)], r_sems, 5 + i, (far, grp))
         )
         send_c[i].start()
-    sims = similarities(0)
     for i in range(4):
         finish(i)
+    sims = similarities(0)
     sims += similarities(1)
     sims += similarities(2)
     sims += similarities(3)

time: 43 us -> 43.5 us (1.012)
  Pallas kernels: 39.4 us -> 39.9 us
    pallas_call x1, Pallas kernels: 39.4 us -> 39.9 us  [plane_shards(): pl.pallas_call(functools.partial(kernel, scale, profile_scale), out_shape...]
where the time goes in v6:
time: 43.5 us; the launch traced here: 43.3 us
  Pallas kernels  39.9 us (92%)
  local copies, waits for them, and re-layouts  2.79 us (6%)
  between operations  0.64 us (1%)
    pallas_call x1, Pallas kernels, plane_shards(): pl.pallas_call(functools.partial(kernel, scale, profile_scale), out_shape...  39.9 us
    unnamed x2, local copies, waits for them, and re-layouts  2.79 us

profile of v6, /device:TPU:0, one launch (start us, length us, event | category | flops | bytes accessed | tf_op | source)
XLA Modules:
  0.0 43.3 jit_solution(2145405078477625929)
XLA Ops:
  0.6 39.9 %shard_map.59 = (f32[2,16,1280]{2,1,0:T(8,128)}, f32[2,16]{1,0:T(2,128)}) custom-call(s32[2]{0:T(128)} %ql_hbm.1, s32[4]{0:T(128)} %tl_hbm.1, bf16[2,128,1280]{2,1,0:T(8,128)(2,1)} %q_hbm.1, bf16[4,128,1280]{2,1,0:T(8,128)(2,1)} %t_hbm.1), custom_call_target="tpu_custom_call" | custom-call | tf_op jit(solution)/shard_map/pallas_call | solution.py:356
  40.5 1.6 %copy.8 = f32[2,16,1280]{2,1,0:T(8,128)} copy(f32[2,16,1280]{2,1,0:T(8,128)} %get-tuple-element.4) | data formatting | bytes 327680
  42.1 1.2 %copy.9 = f32[2,16]{1,0:T(2,128)} copy(f32[2,16]{1,0:T(2,128)} %get-tuple-element.5) | data formatting | bytes 256
